TPU v7x, 128 devices: a whole 4x4x4 slice. The times are simulated.
128 devices in a mesh: tp: 32 (over y, z, x_lo), col: 4 (over x_hi, core).
Axes of the slice: x: 4 (x_hi: 2, x_lo: 2; x = x_hi * 2 + x_lo), y: 4, z: 4, core: 2. Of those that a mesh axis runs over, the one named last changes fastest.
Arguments:
- momentum: float32 [9216, 18432], P('tp', 'col'), may hold values from -2000 to 2000
Outputs:
- gram: float32 [9216, 9216], P('tp', 'col')
All inputs are finite; a program needn't handle non-finite values.
Results may differ from a plain program's by a relative error of at most 0.0022.
Values may be sent and summed in bfloat16 or wider, within the bound.
A program may use at most 192 MiB of HBM per device.

v0:
```python
import jax
import jax.numpy as jnp
from jax import lax
from jax.sharding import PartitionSpec as P


def block_product(left, right):
    return lax.dot_general(
        left, right, (((1,), (1,)), ((), ())), preferred_element_type=jnp.float32
    )


def shards(momentum):
    total = lax.psum(jnp.sum(momentum * momentum), ("tp", "col"))
    normalized = (momentum * (1.0 / (jnp.sqrt(total) + 1e-07))).astype(jnp.bfloat16)
    row_dev = normalized.shape[0]
    count = lax.axis_size("tp")
    partial_band = block_product(normalized, lax.all_gather(normalized, "tp", axis=0, tiled=True))
    summed = lax.psum_scatter(partial_band, "col", scatter_dimension=1, tiled=True)
    return summed * jnp.float32(row_dev * count)


def solution(mesh):
    in_specs = (P("tp", "col"),)
    out_specs = P("tp", "col")
    return jax.shard_map(shards, mesh=mesh, in_specs=in_specs, out_specs=out_specs, check_vma=False)
```

profile of v0, /device:TPU:25, one launch (start us, length us, event | category | flops | bytes accessed | tf_op | source)
XLA Modules:
  0.0 1998.0 jit_solution(10468848822994816751)
XLA Ops:
  6.5 0.0 all-gather.2.cloned.1.call-start
  6.5 4.5 multiply_reduce_fusion
  11.0 65.7 %psum.7 = f32[]{:T(128)} all-reduce(f32[]{:T(128)} %multiply_reduce_fusion), channel_id=1, replica_groups=mesh['tp'=32,'col'=4] {'tp','col'}, use_global_device_ids=true, to_apply=%region_1.0 | all-reduce | flops 1 | bytes 8 | tf_op jit(solution)/shard_map/psum | solution.py:14
  77.5 4.3 multiply_convert_fusion
  81.8 0.0 all-gather.2.cloned.1.call-update
  81.8 0.0 reduce-scatter.2.cloned.1.call-start
  81.9 1773.6 %all-gather.2.cloned.1.call-done = bf16[9216,4608]{1,0:T(8,128)(2,1)} async-done(((bf16[288,4608]{1,0:T(8,128)(2,1)}), bf16[9216,4608]{1,0:T(8,128)(2,1)}) %all-gather.2.cloned.1.call-update) | async-done | bytes 84934672 | tf_op jit(solution)/shard_map/all_gather | solution.py:18
  1855.5 38.0 %fusion = f32[288,9216]{1,0:T(8,128)} fusion(bf16[288,4608]{1,0:T(8,128)(2,1)} %multiply_convert_fusion, bf16[9216,4608]{1,0:T(8,128)(2,1)} %all-gather.2.cloned.1.call-done), kind=kOutput, calls=%fused_computation.3 | convolution fusion | flops 24461180928 | bytes 98205696 | tf_op jit(solution)/shard_map/dot_general | solution.py:8
  1893.5 0.0 reduce-scatter.2.cloned.1.call-update
  1893.5 94.2 %reduce-scatter.2.cloned.1.call-done = f32[288,2304]{1,0:T(8,128)} async-done(((f32[288,9216]{1,0:T(8,128)}), f32[288,2304]{1,0:T(8,128)}) %reduce-scatter.2.cloned.1.call-update) | async-done | bytes 2654224 | tf_op jit(solution)/shard_map/reduce_scatter | solution.py:19
  1987.8 3.4 broadcast_multiply_fusion
Async XLA Ops:
  6.5 1849.0 %all-gather.2.cloned.1.call-start = ((), (), s32[]{:S(2)}) async-start(), calls=%async_computation.1 | async-start | bytes 87588864 | tf_op jit(solution)/shard_map/all_gather | solution.py:18
  81.8 1905.9 %reduce-scatter.2.cloned.1.call-start = ((), (), s32[]{:S(2)}) async-start(), calls=%async_computation.2 | async-start | bytes 13271040 | tf_op jit(solution)/shard_map/reduce_scatter | solution.py:19
Sparse Core Ops, SparseCore 0:
  81.9 1773.5 all-gather.1
  1893.6 94.0 reduce-scatter.1
where the time goes:
time: 2000 us
  waiting for transfers between devices  1870 us (94%)
  blocking collectives  65.7 us (3%)
  matrix products  38 us (2%)
    all_gather x1, waiting for transfers between devices, shards(): lax.all_gather(normalized, 'tp', axis=0, tiled=True)  1770 us
    reduce_scatter x1, waiting for transfers between devices, shards(): lax.psum_scatter(partial_band, 'col', scatter_dimension=1, tiled=True)  94.2 us
    psum x1, blocking collectives, shards(): total = lax.psum(jnp.sum(momentum * momentum), ('tp', 'col'))  65.7 us
  transfers between devices with their start and end apart: 2, of which 2 were waited for; matrix products, arithmetic and copies ran while one was open for 0% of the time, Pallas kernels for 0%

commit v1 on v0

v1 whole, which is shorter than its diff:
```python
import functools

import jax
import jax.numpy as jnp
from jax import lax
from jax.experimental import pallas as pl
from jax.experimental.pallas import tpu as pltpu
from jax.sharding import PartitionSpec as P

SLOTS = ((0, 0), (1, 0), (3, 0), (0, 1), (0, 3), (2, 0), (0, 2))
OWN, Y1, Y3, Z1, Z3, Y2, Z2 = range(7)
PAIRS = (
    (OWN, OWN, False),
    (OWN, Z1, True),
    (Z3, Z1, False),
    (OWN, Y1, True),
    (Z1, Y1, True),
    (Y1, Y3, False),
    (Z1, Y3, True),
    (Z2, Y3, True),
    (Z1, Y2, True),
    (Z2, Y2, False),
)
EARLY = tuple(range(7))
LATE = tuple(range(7, 10))
QUARTER = tuple(tuple(e for e, (_, b, _) in enumerate(PAIRS) if SLOTS[b][0] == q) for q in range(4))
PARITY = tuple(tuple(sorted(QUARTER[p] + QUARTER[p + 2])) for p in range(2))
MESH = pl.DeviceIdType.MESH
F32, BF16 = jnp.float32, jnp.bfloat16
CHUNK = 384


def kernel(
    factor, m_ref, o_ref,
    slots, xsend, acc, d2, xs, xr, fb, ftb, outb, part, g8, gy, gz,
    in_sem, ps_s, ps_r, gat_s, gat_r, fwd_s, xc_s, d2_s, d2_r, x_s, x_r, f_s, f_r,
):
    rows = m_ref.shape[0]
    half = m_ref.shape[1] // 2
    cut = (half // 2) // 256 * 256
    spans = ((0, cut), (cut, half - cut))
    t, c = lax.axis_index("tp"), lax.axis_index("col")
    y, z, r = t // 8, (t // 2) % 4, t % 2
    q = (c - y + 4) % 4
    per_half = half // CHUNK

    def at(dy=0, dz=0, xl=None, dc=0):
        xl = r if xl is None else xl
        return ((((y + dy) % 4) * 4 + (z + dz) % 4) * 2 + xl, (c + dc + 4) % 4)

    core_peer = (t, c + 1 - 2 * (c % 2))
    other = 1 - r

    loads = []
    for j in range(2 * per_half):
        dst = acc.at[j // 2, pl.ds((j % 2) * rows, rows), pl.ds(0, CHUNK)]
        loads.append(pltpu.make_async_copy(m_ref.at[:, pl.ds(j * CHUNK, CHUNK)], dst, in_sem.at[j]))
        loads[-1].start()

    bar = pltpu.get_barrier_semaphore()
    me8 = r * 4 + c

    def at8(i):
        return ((y * 4 + z) * 2 + i // 4, i % 4)

    greet = [at8((me8 + o) % 8) for o in range(1, 8)]
    greet += [at(dy=o) for o in range(1, 4)] + [at(dz=o) for o in range(1, 4)]
    greet += [at(dz=1, xl=other), at(dz=3, xl=other)]
    for dy, dc in ((1, 3), (3, 1), (2, 2)):
        greet += [at(dy=dy, xl=r, dc=dc), at(dy=dy, xl=other, dc=dc)]
    for dev in greet:
        pl.semaphore_signal(bar, inc=1, device_id=dev, device_id_type=MESH)

    total = jnp.zeros((8, CHUNK), F32)
    for j in range(2 * per_half):
        loads[j].wait()
        v = acc[j // 2, (j % 2) * rows : (j % 2 + 1) * rows, 0:CHUNK]
        total += jnp.sum((v * v).reshape(rows // 8, 8, CHUNK), axis=0)
    part[0] = total[:, 0:128] + total[:, 128:256] + total[:, 256:384]
    pl.semaphore_wait(bar, len(greet))
    done = []

    def share(stage, place, me, n, device):
        place[pl.ds(me, 1)] = part[stage][None]
        copies = []
        for o in range(1, n):
            i = 8 * stage + o
            copies.append(
                pltpu.make_async_remote_copy(
                    part.at[stage], place.at[me], ps_s.at[i], ps_r.at[stage, o],
                    device_id=device(o), device_id_type=MESH,
                )
            )
            copies[-1].start()
        for o in range(1, n):
            copies[o - 1].wait_recv()
        done.extend(copies)
        return jnp.sum(place[...], axis=0)

    part[1] = share(0, g8, me8, 8, lambda o: at8((me8 + o) % 8))
    part[2] = share(1, gy, y, 4, lambda o: at(dy=o))
    whole = share(2, gz, z, 4, lambda o: at(dz=o))
    total = jnp.sum(jnp.sum(whole, axis=0, keepdims=True), axis=1, keepdims=True)
    scale = 1.0 / (jnp.sqrt(total) + 1e-07)

    def normalize(which, n0, n1, store):
        for n in range(n0, n1):
            v = acc[which * (per_half // 2) + n // 2, (n % 2) * rows : (n % 2 + 1) * rows, 0:CHUNK]
            store(n, (v * scale).astype(BF16))

    mine = pl.ds(pl.multiple_of(r * rows, 16), rows)
    theirs = pl.ds(pl.multiple_of(other * rows, 16), rows)

    def to_own(n, v):
        slots[OWN, mine, n * CHUNK : (n + 1) * CHUNK] = v

    def to_send(n, v):
        xsend[:, n * CHUNK : (n + 1) * CHUNK] = v

    def unit(slot, rr, k):
        start = pl.ds(pl.multiple_of(rr * rows, 16), rows)
        return slots.at[slot, start, pl.ds(*spans[k])]

    direct = ((Y1, at(dy=3)), (Y3, at(dy=1)), (Z1, at(dz=3)), (Z3, at(dz=1)))

    def send_own(rr, second, k):
        for i, (slot, dev) in enumerate(direct):
            cp = pltpu.make_async_remote_copy(
                unit(OWN, rr, k), unit(slot, rr, k), gat_s.at[i, second, k], gat_r.at[slot, rr, k],
                device_id=dev, device_id_type=MESH,
            )
            cp.start()
            done.append(cp)

    def arrived(slot, rr, k):
        ref = unit(slot, rr, k)
        pltpu.make_async_copy(ref, ref, gat_r.at[slot, rr, k]).wait()

    def send_x(k):
        cp = pltpu.make_async_remote_copy(
            xsend.at[:, pl.ds(*spans[k])], unit(OWN, r, k), xc_s.at[k], gat_r.at[OWN, r, k],
            device_id=at(xl=other), device_id_type=MESH,
        )
        cp.start()
        done.append(cp)

    onward = {Y1: (0, Y2, at(dy=3)), Z1: (1, Z2, at(dz=3)), Y3: (0, Y2, at(dy=1)), Z3: (1, Z2, at(dz=1))}

    def forward(slot, rr, second, k):
        i, to, dev = onward[slot]
        cp = pltpu.make_async_remote_copy(
            unit(slot, rr, k), unit(to, rr, k), fwd_s.at[i, second, k], gat_r.at[to, rr, k],
            device_id=dev, device_id_type=MESH,
        )
        cp.start()
        done.append(cp)

    first_cut = -(-cut // CHUNK)
    normalize(r, 0, first_cut, to_own)
    send_own(r, 0, 0)
    normalize(other, 0, first_cut, to_send)
    send_x(0)
    normalize(other, first_cut, per_half, to_send)
    normalize(r, first_cut, per_half, to_own)
    send_x(1)

    tile = 192

    def product(e, k):
        a, b, _ = PAIRS[e]

        def step(i, _):
            here = pl.ds(pl.multiple_of(i * tile, tile), tile)
            cols = pl.ds(*spans[k])
            p = lax.dot_general(
                slots[a, here, cols], slots[b, :, cols], (((1,), (1,)), ((), ())), preferred_element_type=F32
            )
            if k == 0:
                acc[e, here, :] = p
            else:
                acc[e, here, :] += p
            return 0

        lax.fori_loop(0, 2 * rows // tile, step, 0)

    arrived(OWN, other, 0)
    send_own(other, 1, 0)
    send_own(r, 0, 1)
    arrived(OWN, other, 1)
    send_own(other, 1, 1)
    for slot in (Y1, Z1):
        arrived(slot, r, 0)
        forward(slot, r, 0, 0)
    for slot in (Y1, Z1):
        arrived(slot, other, 0)
        forward(slot, other, 1, 0)
    for slot in (Y3, Z3):
        for rr in (r, other):
            arrived(slot, rr, 0)
    for e in EARLY:
        product(e, 0)
    for slot in (Y3, Z3):
        arrived(slot, r, 1)
        forward(slot, r, 0, 1)
    for slot in (Y3, Z3):
        arrived(slot, other, 1)
        forward(slot, other, 1, 1)
    for slot in (Y1, Z1):
        for rr in (r, other):
            arrived(slot, rr, 1)
    for e in EARLY:
        product(e, 1)

    def branches(body):
        for k in range(4):
            @pl.when(q == k)
            def _(k=k):
                body(k)

    def core_copy(k, e):
        i = PARITY[1 - k % 2].index(e)
        return pltpu.make_async_remote_copy(
            acc.at[e], d2.at[i], d2_s.at[i], d2_r.at[i], device_id=core_peer, device_id_type=MESH
        )

    def to_core(k, group):
        for e in PARITY[1 - k % 2]:
            if e in group:
                core_copy(k, e).start()

    def x_copy(e, i, kind):
        dev = (at(xl=other), at(dc=2), at(xl=other, dc=2))[kind]
        return pltpu.make_async_remote_copy(
            xs.at[i, kind], xr.at[i, kind], x_s.at[i, kind], x_r.at[i, kind], device_id=dev, device_id_type=MESH
        )

    def x_moves(k, group):
        out = []
        for e in PARITY[k % 2]:
            if e in group:
                i = QUARTER[SLOTS[PAIRS[e][1]][0]].index(e)
                if e in QUARTER[k]:
                    out.append((e, i, 0))
                else:
                    out += [(e, i, 1), (e, i, 2)]
        return out

    def to_x(k, group):
        for e in PARITY[k % 2]:
            if e in group:
                i = PARITY[k % 2].index(e)
                pltpu.make_async_copy(d2.at[i], d2.at[i], d2_r.at[i]).wait()
        for e, i, kind in x_moves(k, group):
            where = mine if kind == 1 else theirs
            j = PARITY[k % 2].index(e)
            xs[i, kind] = (acc[e, where, :] + d2[j, where, :]).astype(BF16)
            x_copy(e, i, kind).start()

    def final_copies(k, e):
        a, b, both = PAIRS[e]
        i = QUARTER[k].index(e)
        (ay, az), (by, bz) = SLOTS[a], SLOTS[b]
        copies = []
        if a != OWN:
            for n in range(2):
                copies.append(
                    pltpu.make_async_remote_copy(
                        fb.at[i, n], outb.at[(z + bz) % 4, n], f_s.at[i, n], f_r.at[(z + bz) % 4, n],
                        device_id=at(ay, az), device_id_type=MESH,
                    )
                )
        if both:
            for n in range(2):
                copies.append(
                    pltpu.make_async_remote_copy(
                        ftb.at[i, n], outb.at[(z + az) % 4, r], f_s.at[i, 2 + n], f_r.at[(z + az) % 4, r],
                        device_id=at(by, bz, xl=n, dc=ay - by), device_id_type=MESH,
                    )
                )
        return copies

    def to_final(k, group):
        for e in QUARTER[k]:
            if e not in group:
                continue
            a, b, both = PAIRS[e]
            i = QUARTER[k].index(e)
            j = PARITY[k % 2].index(e)
            for kind in range(3):
                pltpu.make_async_copy(xr.at[i, kind], xr.at[i, kind], x_r.at[i, kind]).wait()
            v = acc[e, mine, :] + d2[j, mine, :]
            for kind in range(3):
                v += xr[i, kind].astype(F32)
            v *= factor
            bz = SLOTS[b][1]
            for n in range(2):
                w = v[:, n * rows : (n + 1) * rows]
                if a == OWN:
                    outb[(z + bz) % 4, n] = w
                else:
                    fb[i, n] = w
                if both:
                    ftb[i, n] = w.T
            for cp in final_copies(k, e):
                cp.start()

    branches(lambda k: to_core(k, EARLY))
    branches(lambda k: to_x(k, EARLY))
    for k in range(2):
        for slot in (Y2, Z2):
            for rr in (r, other):
                arrived(slot, rr, k)
        for e in LATE:
            product(e, k)
    branches(lambda k: to_core(k, LATE))
    branches(lambda k: to_x(k, LATE))
    branches(lambda k: to_final(k, EARLY))
    branches(lambda k: to_final(k, LATE))

    local = ((0, 1), (0,), (), ())

    def finish(k):
        for dz in range(4):
            if dz not in local[k]:
                for n in range(2):
                    ref = outb.at[(z + dz) % 4, n]
                    pltpu.make_async_copy(ref, ref, f_r.at[(z + dz) % 4, n]).wait()

    branches(finish)
    for i in range(8):
        o_ref[:, i * rows : (i + 1) * rows] = outb[i // 2, i % 2]

    for cp in done:
        cp.wait_send()

    def drain(k):
        for e in PARITY[1 - k % 2]:
            core_copy(k, e).wait_send()
        for e, i, kind in x_moves(k, EARLY + LATE):
            x_copy(e, i, kind).wait_send()
        for e in QUARTER[k]:
            for cp in final_copies(k, e):
                cp.wait_send()

    branches(drain)


def gram(momentum):
    rows, cols = momentum.shape
    half = cols // 2
    n_rows = rows * lax.axis_size("tp")
    most = max(len(s) for s in QUARTER)
    dma = pltpu.SemaphoreType.DMA
    return pl.pallas_call(
        functools.partial(kernel, float(n_rows)),
        out_shape=jax.ShapeDtypeStruct((rows, 8 * rows), F32),
        in_specs=[pl.BlockSpec(memory_space=pl.ANY)],
        out_specs=pl.BlockSpec(memory_space=pltpu.VMEM),
        scratch_shapes=[
            pltpu.VMEM((len(SLOTS), 2 * rows, half), BF16),
            pltpu.VMEM((rows, half), BF16),
            pltpu.VMEM((len(PAIRS), 2 * rows, 2 * rows), F32),
            pltpu.VMEM((5, 2 * rows, 2 * rows), F32),
            pltpu.VMEM((most, 3, rows, 2 * rows), BF16),
            pltpu.VMEM((most, 3, rows, 2 * rows), BF16),
            pltpu.VMEM((most, 2, rows, rows), F32),
            pltpu.VMEM((most, 2, rows, rows), F32),
            pltpu.VMEM((4, 2, rows, rows), F32),
            pltpu.VMEM((3, 8, 128), F32),
            pltpu.VMEM((8, 8, 128), F32),
            pltpu.VMEM((4, 8, 128), F32),
            pltpu.VMEM((4, 8, 128), F32),
            dma((cols // CHUNK,)),
            dma((24,)),
            dma((3, 8)),
            dma((4, 2, 2)),
            dma((len(SLOTS), 2, 2)),
            dma((2, 2, 2)),
            dma((2,)),
            dma((5,)),
            dma((5,)),
            dma((most, 3)),
            dma((most, 3)),
            dma((most, 4)),
            dma((4, 2)),
        ],
        compiler_params=pltpu.CompilerParams(
            collective_id=0, has_side_effects=True, vmem_limit_bytes=62 * 2**20
        ),
        cost_estimate=pl.CostEstimate(
            flops=2 * 10 * (2 * rows) ** 2 * half, bytes_accessed=4 * rows * (cols + 8 * rows), transcendentals=0
        ),
    )(momentum)


def solution(mesh):
    return jax.shard_map(gram, mesh=mesh, in_specs=(P("tp", "col"),), out_specs=P("tp", "col"), check_vma=False)
```

time: 2000 us -> 185 us (0.09)
  waiting for transfers between devices: 1870 us -> 0 us
  Pallas kernels: 0 us -> 178 us
  blocking collectives: 65.7 us -> 0 us
  matrix products: 38 us -> 0 us
    all_gather x1 -> x0, waiting for transfers between devices: 1770 us -> none  [shards(): lax.all_gather(normalized, 'tp', axis=0, tiled=True)]
    pallas_call x0 -> x1, Pallas kernels: none -> 178 us  [gram(): pl.pallas_call(functools.partial(kernel, float(n_rows)), out_shape=jax.Sh...]
    reduce_scatter x1 -> x0, waiting for transfers between devices: 94.2 us -> none  [shards(): lax.psum_scatter(partial_band, 'col', scatter_dimension=1, tiled=True)]
    psum x1 -> x0, blocking collectives: 65.7 us -> none  [shards(): total = lax.psum(jnp.sum(momentum * momentum), ('tp', 'col'))]
    dot_general x1 -> x0, matrix products: 38 us -> none  [block_product(): lax.dot_general(left, right, (((1,), (1,)), ((), ())), preferred_element_...]
  transfers between devices with their start and end apart: 2 -> 0, of which waited for: 2 -> 0; matrix products, arithmetic and copies ran while one was open for 0% -> 0% of each run, Pallas kernels for 0% -> 0%
where the time goes in v1:
time: 185 us; the launch traced here: 182 us
  Pallas kernels  178 us (96%)
  local copies, waits for them, and re-layouts  3.42 us (2%)
    pallas_call x1, Pallas kernels, gram(): pl.pallas_call(functools.partial(kernel, float(n_rows)), out_shape=jax.Sh...  178 us

profile of v1, /device:TPU:25, one launch (start us, length us, event | category | flops | bytes accessed | tf_op | source)
XLA Modules:
  0.0 181.8 jit_solution(2917113466619095187)
XLA Ops:
  0.0 178.4 %shard_map.17 = f32[288,2304]{1,0:T(8,128)} custom-call(f32[288,4608]{1,0:T(8,128)} %m_ref.1), custom_call_target="tpu_custom_call" | custom-call | flops 15288238080 | bytes 7962624 | tf_op jit(solution)/shard_map/pallas_call | solution.py:354
  178.4 3.4 %copy.3 = f32[288,2304]{1,0:T(8,128)} copy(f32[288,2304]{1,0:T(8,128)} %shard_map.17) | data formatting | bytes 5308416

commit v2 on v1

--- a/solution.py
+++ b/solution.py
@@ -18,11 +18,9 @@
     (Y1, Y3, False),
     (Z1, Y3, True),
     (Z2, Y3, True),
-    (Z1, Y2, True),
+    (Y2, Z1, True),
     (Z2, Y2, False),
 )
-EARLY = tuple(range(7))
-LATE = tuple(range(7, 10))
 QUARTER = tuple(tuple(e for e, (_, b, _) in enumerate(PAIRS) if SLOTS[b][0] == q) for q in range(4))
 PARITY = tuple(tuple(sorted(QUARTER[p] + QUARTER[p + 2])) for p in range(2))
 MESH = pl.DeviceIdType.MESH
@@ -162,16 +160,18 @@
     send_x(0)
     normalize(other, first_cut, per_half, to_send)
     normalize(r, first_cut, per_half, to_own)
-    send_x(1)
 
     tile = 192
 
-    def product(e, k):
+    def product(e, k, rr=None):
         a, b, _ = PAIRS[e]
+        cols = pl.ds(*spans[k])
+        size = tile if rr is None else tile // 2
+        base = 0 if rr is None else rr * rows
+        n = 2 * rows // tile
 
         def step(i, _):
-            here = pl.ds(pl.multiple_of(i * tile, tile), tile)
-            cols = pl.ds(*spans[k])
+            here = pl.ds(pl.multiple_of(base + i * size, size), size)
             p = lax.dot_general(
                 slots[a, here, cols], slots[b, :, cols], (((1,), (1,)), ((), ())), preferred_element_type=F32
             )
@@ -181,35 +181,14 @@
                 acc[e, here, :] += p
             return 0
 
-        lax.fori_loop(0, 2 * rows // tile, step, 0)
+        lax.fori_loop(0, n, step, 0)
 
     arrived(OWN, other, 0)
+    send_x(1)
     send_own(other, 1, 0)
     send_own(r, 0, 1)
     arrived(OWN, other, 1)
     send_own(other, 1, 1)
-    for slot in (Y1, Z1):
-        arrived(slot, r, 0)
-        forward(slot, r, 0, 0)
-    for slot in (Y1, Z1):
-        arrived(slot, other, 0)
-        forward(slot, other, 1, 0)
-    for slot in (Y3, Z3):
-        for rr in (r, other):
-            arrived(slot, rr, 0)
-    for e in EARLY:
-        product(e, 0)
-    for slot in (Y3, Z3):
-        arrived(slot, r, 1)
-        forward(slot, r, 0, 1)
-    for slot in (Y3, Z3):
-        arrived(slot, other, 1)
-        forward(slot, other, 1, 1)
-    for slot in (Y1, Z1):
-        for rr in (r, other):
-            arrived(slot, rr, 1)
-    for e in EARLY:
-        product(e, 1)
 
     def branches(body):
         for k in range(4):
@@ -223,10 +202,12 @@
             acc.at[e], d2.at[i], d2_s.at[i], d2_r.at[i], device_id=core_peer, device_id_type=MESH
         )
 
-    def to_core(k, group):
-        for e in PARITY[1 - k % 2]:
-            if e in group:
+    def to_core(e):
+        def body(k):
+            if e in PARITY[1 - k % 2]:
                 core_copy(k, e).start()
+
+        branches(body)
 
     def x_copy(e, i, kind):
         dev = (at(xl=other), at(dc=2), at(xl=other, dc=2))[kind]
@@ -234,27 +215,31 @@
             xs.at[i, kind], xr.at[i, kind], x_s.at[i, kind], x_r.at[i, kind], device_id=dev, device_id_type=MESH
         )
 
-    def x_moves(k, group):
-        out = []
-        for e in PARITY[k % 2]:
-            if e in group:
-                i = QUARTER[SLOTS[PAIRS[e][1]][0]].index(e)
-                if e in QUARTER[k]:
-                    out.append((e, i, 0))
-                else:
-                    out += [(e, i, 1), (e, i, 2)]
-        return out
-
-    def to_x(k, group):
-        for e in PARITY[k % 2]:
-            if e in group:
-                i = PARITY[k % 2].index(e)
-                pltpu.make_async_copy(d2.at[i], d2.at[i], d2_r.at[i]).wait()
-        for e, i, kind in x_moves(k, group):
-            where = mine if kind == 1 else theirs
+    def x_moves(k, e):
+        if e in QUARTER[k]:
+            return [(QUARTER[k].index(e), 0)]
+        i = QUARTER[(k + 2) % 4].index(e)
+        return [(i, 1), (i, 2)]
+
+    short = rows // 2
+
+    def band(rr, n):
+        return pl.ds(pl.multiple_of(rr * rows + n * short, 16), short)
+
+    def to_x(e):
+        def body(k):
+            if e not in PARITY[k % 2]:
+                return
             j = PARITY[k % 2].index(e)
-            xs[i, kind] = (acc[e, where, :] + d2[j, where, :]).astype(BF16)
-            x_copy(e, i, kind).start()
+            pltpu.make_async_copy(d2.at[j], d2.at[j], d2_r.at[j]).wait()
+            for i, kind in x_moves(k, e):
+                rr = r if kind == 1 else other
+                for n in range(2):
+                    v = acc[e, band(rr, n), :] + d2[j, band(rr, n), :]
+                    xs[i, kind, :, n * 2 * rows : (n + 1) * 2 * rows] = v.astype(BF16)
+                x_copy(e, i, kind).start()
+
+        branches(body)
 
     def final_copies(k, e):
         a, b, both = PAIRS[e]
@@ -279,43 +264,81 @@
                 )
         return copies
 
-    def to_final(k, group):
-        for e in QUARTER[k]:
-            if e not in group:
-                continue
+    quart = rows // 4
+
+    def fold(ref, v, first=0):
+        for n in range(v.shape[0] // quart):
+            ref[:, (first + n) * rows : (first + n + 1) * rows] = v[n * quart : (n + 1) * quart]
+
+    def to_final(e):
+        def body(k):
+            if e not in QUARTER[k]:
+                return
             a, b, both = PAIRS[e]
             i = QUARTER[k].index(e)
             j = PARITY[k % 2].index(e)
             for kind in range(3):
                 pltpu.make_async_copy(xr.at[i, kind], xr.at[i, kind], x_r.at[i, kind]).wait()
-            v = acc[e, mine, :] + d2[j, mine, :]
-            for kind in range(3):
-                v += xr[i, kind].astype(F32)
-            v *= factor
+            parts = []
+            for n in range(2):
+                v = acc[e, band(r, n), :] + d2[j, band(r, n), :]
+                for kind in range(3):
+                    v += xr[i, kind, :, n * 2 * rows : (n + 1) * 2 * rows].astype(F32)
+                parts.append(v * factor)
             bz = SLOTS[b][1]
             for n in range(2):
-                w = v[:, n * rows : (n + 1) * rows]
-                if a == OWN:
-                    outb[(z + bz) % 4, n] = w
-                else:
-                    fb[i, n] = w
+                w = [v[:, n * rows : (n + 1) * rows] for v in parts]
+                ref = outb.at[(z + bz) % 4, n] if a == OWN else fb.at[i, n]
+                fold(ref, w[0])
+                fold(ref, w[1], 2)
                 if both:
-                    ftb[i, n] = w.T
+                    fold(ftb.at[i, n], jnp.concatenate(w, axis=0).T)
             for cp in final_copies(k, e):
                 cp.start()
 
-    branches(lambda k: to_core(k, EARLY))
-    branches(lambda k: to_x(k, EARLY))
+        branches(body)
+
     for k in range(2):
-        for slot in (Y2, Z2):
-            for rr in (r, other):
+        product(0, k)
+    to_core(0)
+    for slot in (Y1, Z1, Y3, Z3):
+        for rr in (r, other):
+            arrived(slot, rr, 0)
+    to_x(0)
+    early = (4, 6, 3, 5, 1, 2)
+    for e in early:
+        product(e, 0)
+    for slot in (Y1, Z1, Y3, Z3):
+        for rr in (r, other):
+            arrived(slot, rr, 1)
+    for n, rr in enumerate((r, other)):
+        for slot in (Y1, Z1):
+            forward(slot, rr, n, 0)
+        for slot in (Y3, Z3):
+            forward(slot, rr, n, 1)
+    for n, e in enumerate(early):
+        product(e, 1)
+        to_core(e)
+        if n:
+            to_x(early[n - 1])
+    to_x(early[-1])
+    to_final(0)
+    for rr in (r, other):
+        for slot in (Z2, Y2):
+            for k in range(2):
                 arrived(slot, rr, k)
-        for e in LATE:
-            product(e, k)
-    branches(lambda k: to_core(k, LATE))
-    branches(lambda k: to_x(k, LATE))
-    branches(lambda k: to_final(k, EARLY))
-    branches(lambda k: to_final(k, LATE))
+        for e in (7, 8):
+            for k in range(2):
+                product(e, k, rr)
+    to_core(7)
+    to_core(8)
+    for k in range(2):
+        product(9, k)
+    to_core(9)
+    for e in (7, 8, 9):
+        to_x(e)
+    for e in early + (7, 8, 9):
+        to_final(e)
 
     local = ((0, 1), (0,), (), ())
 
@@ -328,7 +351,10 @@
 
     branches(finish)
     for i in range(8):
-        o_ref[:, i * rows : (i + 1) * rows] = outb[i // 2, i % 2]
+        for n in range(4):
+            o_ref[n * quart : (n + 1) * quart, i * rows : (i + 1) * rows] = outb[
+                i // 2, i % 2, :, n * rows : (n + 1) * rows
+            ]
 
     for cp in done:
         cp.wait_send()
@@ -336,8 +362,9 @@
     def drain(k):
         for e in PARITY[1 - k % 2]:
             core_copy(k, e).wait_send()
-        for e, i, kind in x_moves(k, EARLY + LATE):
-            x_copy(e, i, kind).wait_send()
+        for e in PARITY[k % 2]:
+            for i, kind in x_moves(k, e):
+                x_copy(e, i, kind).wait_send()
         for e in QUARTER[k]:
             for cp in final_copies(k, e):
                 cp.wait_send()
@@ -361,11 +388,11 @@
             pltpu.VMEM((rows, half), BF16),
             pltpu.VMEM((len(PAIRS), 2 * rows, 2 * rows), F32),
             pltpu.VMEM((5, 2 * rows, 2 * rows), F32),
-            pltpu.VMEM((most, 3, rows, 2 * rows), BF16),
-            pltpu.VMEM((most, 3, rows, 2 * rows), BF16),
-            pltpu.VMEM((most, 2, rows, rows), F32),
-            pltpu.VMEM((most, 2, rows, rows), F32),
-            pltpu.VMEM((4, 2, rows, rows), F32),
+            pltpu.VMEM((most, 3, rows // 2, 4 * rows), BF16),
+            pltpu.VMEM((most, 3, rows // 2, 4 * rows), BF16),
+            pltpu.VMEM((most, 2, rows // 4, 4 * rows), F32),
+            pltpu.VMEM((most, 2, rows // 4, 4 * rows), F32),
+            pltpu.VMEM((4, 2, rows // 4, 4 * rows), F32),
             pltpu.VMEM((3, 8, 128), F32),
             pltpu.VMEM((8, 8, 128), F32),
             pltpu.VMEM((4, 8, 128), F32),

time: 185 us -> 165 us (0.89); the launches traced: 182 us -> 165 us
  Pallas kernels: 178 us -> 162 us
    pallas_call x1, Pallas kernels: 178 us -> 162 us  [gram(): pl.pallas_call(functools.partial(kernel, float(n_rows)), out_shape=jax.Sh...]
where the time goes in v2:
time: 165 us
  Pallas kernels  162 us (98%)
  local copies, waits for them, and re-layouts  3.42 us (2%)
    pallas_call x1, Pallas kernels, gram(): pl.pallas_call(functools.partial(kernel, float(n_rows)), out_shape=jax.Sh...  162 us
    unnamed x1, local copies, waits for them, and re-layouts  3.42 us

profile of v2, /device:TPU:25, one launch (start us, length us, event | category | flops | bytes accessed | tf_op | source)
XLA Modules:
  0.0 165.3 jit_solution(6540906286892178141)
XLA Ops:
  0.0 161.8 %shard_map.17 = f32[288,2304]{1,0:T(8,128)} custom-call(f32[288,4608]{1,0:T(8,128)} %m_ref.1), custom_call_target="tpu_custom_call" | custom-call | flops 15288238080 | bytes 7962624 | tf_op jit(solution)/shard_map/pallas_call | solution.py:381
  161.9 3.4 %copy.3 = f32[288,2304]{1,0:T(8,128)} copy(f32[288,2304]{1,0:T(8,128)} %shard_map.17) | data formatting | bytes 5308416

commit v3 on v2

--- a/solution.py
+++ b/solution.py
@@ -10,19 +10,20 @@
 SLOTS = ((0, 0), (1, 0), (3, 0), (0, 1), (0, 3), (2, 0), (0, 2))
 OWN, Y1, Y3, Z1, Z3, Y2, Z2 = range(7)
 PAIRS = (
-    (OWN, OWN, False),
-    (OWN, Z1, True),
-    (Z3, Z1, False),
-    (OWN, Y1, True),
-    (Z1, Y1, True),
-    (Y1, Y3, False),
-    (Z1, Y3, True),
-    (Z2, Y3, True),
-    (Y2, Z1, True),
-    (Z2, Y2, False),
+    (OWN, OWN, False, 0),
+    (OWN, Z1, True, 0),
+    (Z3, Z1, False, 2),
+    (OWN, Y1, True, 1),
+    (Z1, Y1, True, 1),
+    (Y1, Y3, False, 3),
+    (Z1, Y3, True, 3),
+    (Z2, Y3, True, 3),
+    (Z1, Y2, True, 2),
+    (Y2, Z2, False, 0),
 )
-QUARTER = tuple(tuple(e for e, (_, b, _) in enumerate(PAIRS) if SLOTS[b][0] == q) for q in range(4))
+QUARTER = tuple(tuple(e for e, p in enumerate(PAIRS) if p[3] == q) for q in range(4))
 PARITY = tuple(tuple(sorted(QUARTER[p] + QUARTER[p + 2])) for p in range(2))
+SENT = tuple(tuple(e for e in q if e) for q in QUARTER)
 MESH = pl.DeviceIdType.MESH
 F32, BF16 = jnp.float32, jnp.bfloat16
 CHUNK = 384
@@ -30,7 +31,7 @@
 
 def kernel(
     factor, m_ref, o_ref,
-    slots, xsend, acc, d2, xs, xr, fb, ftb, outb, part, g8, gy, gz,
+    slots, xsend, acc, d2, xs, xr, fb, ftb, got, outb, part, g8, gy, gz,
     in_sem, ps_s, ps_r, gat_s, gat_r, fwd_s, xc_s, d2_s, d2_r, x_s, x_r, f_s, f_r,
 ):
     rows = m_ref.shape[0]
@@ -63,7 +64,7 @@
 
     greet = [at8((me8 + o) % 8) for o in range(1, 8)]
     greet += [at(dy=o) for o in range(1, 4)] + [at(dz=o) for o in range(1, 4)]
-    greet += [at(dz=1, xl=other), at(dz=3, xl=other)]
+    greet += [at(dz=1, xl=other), at(dz=3, xl=other), at(dz=1, dc=2), at(dz=3, dc=2)]
     for dy, dc in ((1, 3), (3, 1), (2, 2)):
         greet += [at(dy=dy, xl=r, dc=dc), at(dy=dy, xl=other, dc=dc)]
     for dev in greet:
@@ -164,7 +165,7 @@
     tile = 192
 
     def product(e, k, rr=None):
-        a, b, _ = PAIRS[e]
+        a, b = PAIRS[e][:2]
         cols = pl.ds(*spans[k])
         size = tile if rr is None else tile // 2
         base = 0 if rr is None else rr * rows
@@ -242,39 +243,43 @@
         branches(body)
 
     def final_copies(k, e):
-        a, b, both = PAIRS[e]
-        i = QUARTER[k].index(e)
+        a, b, both, q_e = PAIRS[e]
+        i = SENT[k].index(e)
         (ay, az), (by, bz) = SLOTS[a], SLOTS[b]
         copies = []
         if a != OWN:
             for n in range(2):
                 copies.append(
                     pltpu.make_async_remote_copy(
-                        fb.at[i, n], outb.at[(z + bz) % 4, n], f_s.at[i, n], f_r.at[(z + bz) % 4, n],
-                        device_id=at(ay, az), device_id_type=MESH,
+                        fb.at[i, n], got.at[(z + bz) % 4, n], f_s.at[i, n], f_r.at[(z + bz) % 4, n],
+                        device_id=at(ay, az, dc=by - q_e), device_id_type=MESH,
                     )
                 )
         if both:
             for n in range(2):
                 copies.append(
                     pltpu.make_async_remote_copy(
-                        ftb.at[i, n], outb.at[(z + az) % 4, r], f_s.at[i, 2 + n], f_r.at[(z + az) % 4, r],
-                        device_id=at(by, bz, xl=n, dc=ay - by), device_id_type=MESH,
+                        ftb.at[i, n], got.at[(z + az) % 4, r], f_s.at[i, 2 + n], f_r.at[(z + az) % 4, r],
+                        device_id=at(by, bz, xl=n, dc=ay - q_e), device_id_type=MESH,
                     )
                 )
         return copies
 
     quart = rows // 4
 
-    def fold(ref, v, first=0):
-        for n in range(v.shape[0] // quart):
-            ref[:, (first + n) * rows : (first + n + 1) * rows] = v[n * quart : (n + 1) * quart]
+    def fold(ref, w):
+        for m in range(4):
+            ref[:, m * rows : (m + 1) * rows] = w[m // 2][(m % 2) * quart : (m % 2 + 1) * quart]
+
+    def pair_up(ref, w):
+        for m in range(2):
+            ref[:, m * rows : (m + 1) * rows] = w[m].astype(BF16)
 
     def to_final(e):
         def body(k):
             if e not in QUARTER[k]:
                 return
-            a, b, both = PAIRS[e]
+            a, b, both, _ = PAIRS[e]
             i = QUARTER[k].index(e)
             j = PARITY[k % 2].index(e)
             for kind in range(3):
@@ -286,15 +291,19 @@
                     v += xr[i, kind, :, n * 2 * rows : (n + 1) * 2 * rows].astype(F32)
                 parts.append(v * factor)
             bz = SLOTS[b][1]
+            f = SENT[k].index(e) if e else None
             for n in range(2):
                 w = [v[:, n * rows : (n + 1) * rows] for v in parts]
-                ref = outb.at[(z + bz) % 4, n] if a == OWN else fb.at[i, n]
-                fold(ref, w[0])
-                fold(ref, w[1], 2)
+                if a == OWN:
+                    fold(outb.at[(z + bz) % 4, n], w)
+                else:
+                    pair_up(fb.at[f, n], w)
                 if both:
-                    fold(ftb.at[i, n], jnp.concatenate(w, axis=0).T)
-            for cp in final_copies(k, e):
-                cp.start()
+                    turned = jnp.concatenate(w, axis=0).T
+                    pair_up(ftb.at[f, n], (turned[:short], turned[short:]))
+            if e:
+                for cp in final_copies(k, e):
+                    cp.start()
 
         branches(body)
 
@@ -324,19 +333,22 @@
     to_x(early[-1])
     to_final(0)
     for rr in (r, other):
-        for slot in (Z2, Y2):
-            for k in range(2):
-                arrived(slot, rr, k)
-        for e in (7, 8):
-            for k in range(2):
-                product(e, k, rr)
+        for k in range(2):
+            arrived(Z2, rr, k)
+        for k in range(2):
+            product(7, k, rr)
     to_core(7)
+    for k in range(2):
+        for rr in (r, other):
+            arrived(Y2, rr, k)
+        product(8, k)
     to_core(8)
+    to_x(7)
     for k in range(2):
         product(9, k)
     to_core(9)
-    for e in (7, 8, 9):
-        to_x(e)
+    to_x(8)
+    to_x(9)
     for e in early + (7, 8, 9):
         to_final(e)
 
@@ -344,10 +356,13 @@
 
     def finish(k):
         for dz in range(4):
-            if dz not in local[k]:
-                for n in range(2):
-                    ref = outb.at[(z + dz) % 4, n]
-                    pltpu.make_async_copy(ref, ref, f_r.at[(z + dz) % 4, n]).wait()
+            if dz in local[k]:
+                continue
+            for n in range(2):
+                ref = got.at[(z + dz) % 4, n]
+                pltpu.make_async_copy(ref, ref, f_r.at[(z + dz) % 4, n]).wait()
+                v = ref[...].astype(F32)
+                fold(outb.at[(z + dz) % 4, n], (v[:, 0:rows], v[:, rows : 2 * rows]))
 
     branches(finish)
     for i in range(8):
@@ -366,8 +381,9 @@
             for i, kind in x_moves(k, e):
                 x_copy(e, i, kind).wait_send()
         for e in QUARTER[k]:
-            for cp in final_copies(k, e):
-                cp.wait_send()
+            if e:
+                for cp in final_copies(k, e):
+                    cp.wait_send()
 
     branches(drain)
 
@@ -377,6 +393,7 @@
     half = cols // 2
     n_rows = rows * lax.axis_size("tp")
     most = max(len(s) for s in QUARTER)
+    sent = max(len(s) for s in SENT)
     dma = pltpu.SemaphoreType.DMA
     return pl.pallas_call(
         functools.partial(kernel, float(n_rows)),
@@ -390,8 +407,9 @@
             pltpu.VMEM((5, 2 * rows, 2 * rows), F32),
             pltpu.VMEM((most, 3, rows // 2, 4 * rows), BF16),
             pltpu.VMEM((most, 3, rows // 2, 4 * rows), BF16),
-            pltpu.VMEM((most, 2, rows // 4, 4 * rows), F32),
-            pltpu.VMEM((most, 2, rows // 4, 4 * rows), F32),
+            pltpu.VMEM((sent, 2, rows // 2, 2 * rows), BF16),
+            pltpu.VMEM((sent, 2, rows // 2, 2 * rows), BF16),
+            pltpu.VMEM((4, 2, rows // 2, 2 * rows), BF16),
             pltpu.VMEM((4, 2, rows // 4, 4 * rows), F32),
             pltpu.VMEM((3, 8, 128), F32),
             pltpu.VMEM((8, 8, 128), F32),
@@ -408,7 +426,7 @@
             dma((5,)),
             dma((most, 3)),
             dma((most, 3)),
-            dma((most, 4)),
+            dma((sent, 4)),
             dma((4, 2)),
         ],
         compiler_params=pltpu.CompilerParams(

time: 165 us -> 160 us (0.970)
  Pallas kernels: 162 us -> 156 us
    pallas_call x1, Pallas kernels: 162 us -> 156 us  [gram(): pl.pallas_call(functools.partial(kernel, float(n_rows)), out_shape=jax.Sh...]
where the time goes in v3:
time: 160 us
  Pallas kernels  156 us (98%)
  local copies, waits for them, and re-layouts  3.42 us (2%)
    pallas_call x1, Pallas kernels, gram(): pl.pallas_call(functools.partial(kernel, float(n_rows)), out_shape=jax.Sh...  156 us
    unnamed x1, local copies, waits for them, and re-layouts  3.42 us

profile of v3, /device:TPU:25, one launch (start us, length us, event | category | flops | bytes accessed | tf_op | source)
XLA Modules:
  0.0 159.6 jit_solution(12393279185830083043)
XLA Ops:
  0.0 156.1 %shard_map.17 = f32[288,2304]{1,0:T(8,128)} custom-call(f32[288,4608]{1,0:T(8,128)} %m_ref.1), custom_call_target="tpu_custom_call" | custom-call | flops 15288238080 | bytes 7962624 | tf_op jit(solution)/shard_map/pallas_call | solution.py:398
  156.1 3.4 %copy.3 = f32[288,2304]{1,0:T(8,128)} copy(f32[288,2304]{1,0:T(8,128)} %shard_map.17) | data formatting | bytes 5308416

commit v4 on v3

--- a/solution.py
+++ b/solution.py
@@ -332,6 +332,8 @@
             to_x(early[n - 1])
     to_x(early[-1])
     to_final(0)
+    for e in early[:4]:
+        to_final(e)
     for rr in (r, other):
         for k in range(2):
             arrived(Z2, rr, k)
@@ -344,12 +346,14 @@
         product(8, k)
     to_core(8)
     to_x(7)
+    for e in early[4:]:
+        to_final(e)
     for k in range(2):
         product(9, k)
     to_core(9)
     to_x(8)
     to_x(9)
-    for e in early + (7, 8, 9):
+    for e in (7, 8, 9):
         to_final(e)
 
     local = ((0, 1), (0,), (), ())

time: 160 us -> 155 us (0.969)
  Pallas kernels: 156 us -> 151 us
    pallas_call x1, Pallas kernels: 156 us -> 151 us  [gram(): pl.pallas_call(functools.partial(kernel, float(n_rows)), out_shape=jax.Sh...]
where the time goes in v4:
time: 155 us
  Pallas kernels  151 us (97%)
  local copies, waits for them, and re-layouts  3.42 us (2%)
    pallas_call x1, Pallas kernels, gram(): pl.pallas_call(functools.partial(kernel, float(n_rows)), out_shape=jax.Sh...  151 us
    unnamed x1, local copies, waits for them, and re-layouts  3.42 us

profile of v4, /device:TPU:25, one launch (start us, length us, event | category | flops | bytes accessed | tf_op | source)
XLA Modules:
  0.0 154.6 jit_solution(1599286467510957302)
XLA Ops:
  0.0 151.2 %shard_map.17 = f32[288,2304]{1,0:T(8,128)} custom-call(f32[288,4608]{1,0:T(8,128)} %m_ref.1), custom_call_target="tpu_custom_call" | custom-call | flops 15288238080 | bytes 7962624 | tf_op jit(solution)/shard_map/pallas_call | solution.py:402
  151.2 3.4 %copy.3 = f32[288,2304]{1,0:T(8,128)} copy(f32[288,2304]{1,0:T(8,128)} %shard_map.17) | data formatting | bytes 5308416

commit v5 on v4

--- a/solution.py
+++ b/solution.py
@@ -314,7 +314,7 @@
         for rr in (r, other):
             arrived(slot, rr, 0)
     to_x(0)
-    early = (4, 6, 3, 5, 1, 2)
+    early = (2, 6, 4, 5, 3, 1)
     for e in early:
         product(e, 0)
     for slot in (Y1, Z1, Y3, Z3):

time: 155 us -> 154 us (level)
  Pallas kernels: 151 us -> 149 us
    pallas_call x1, Pallas kernels: 151 us -> 149 us  [gram(): pl.pallas_call(functools.partial(kernel, float(n_rows)), out_shape=jax.Sh...]
where the time goes in v5:
time: 154 us; the launch traced here: 152 us
  Pallas kernels  149 us (97%)
  local copies, waits for them, and re-layouts  3.42 us (2%)
    pallas_call x1, Pallas kernels, gram(): pl.pallas_call(functools.partial(kernel, float(n_rows)), out_shape=jax.Sh...  149 us
    unnamed x1, local copies, waits for them, and re-layouts  3.42 us

profile of v5, /device:TPU:25, one launch (start us, length us, event | category | flops | bytes accessed | tf_op | source)
XLA Modules:
  0.0 152.1 jit_solution(16128123137804855187)
XLA Ops:
  0.0 148.6 %shard_map.17 = f32[288,2304]{1,0:T(8,128)} custom-call(f32[288,4608]{1,0:T(8,128)} %m_ref.1), custom_call_target="tpu_custom_call" | custom-call | flops 15288238080 | bytes 7962624 | tf_op jit(solution)/shard_map/pallas_call | solution.py:402
  148.6 3.4 %copy.3 = f32[288,2304]{1,0:T(8,128)} copy(f32[288,2304]{1,0:T(8,128)} %shard_map.17) | data formatting | bytes 5308416

commit v6 on v5

--- a/solution.py
+++ b/solution.py
@@ -346,12 +346,12 @@
         product(8, k)
     to_core(8)
     to_x(7)
-    for e in early[4:]:
-        to_final(e)
     for k in range(2):
         product(9, k)
     to_core(9)
     to_x(8)
+    for e in early[4:]:
+        to_final(e)
     to_x(9)
     for e in (7, 8, 9):
         to_final(e)

time: 154 us -> 154 us (level)
  no operation moved by 1% of the time
where the time goes in v6:
time: 154 us; the launch traced here: 153 us
  Pallas kernels  150 us (97%)
  local copies, waits for them, and re-layouts  3.42 us (2%)
    pallas_call x1, Pallas kernels, gram(): pl.pallas_call(functools.partial(kernel, float(n_rows)), out_shape=jax.Sh...  150 us
    unnamed x1, local copies, waits for them, and re-layouts  3.42 us

profile of v6, /device:TPU:25, one launch (start us, length us, event | category | flops | bytes accessed | tf_op | source)
XLA Modules:
  0.0 153.5 jit_solution(881224182914630815)
XLA Ops:
  0.0 150.0 %shard_map.17 = f32[288,2304]{1,0:T(8,128)} custom-call(f32[288,4608]{1,0:T(8,128)} %m_ref.1), custom_call_target="tpu_custom_call" | custom-call | flops 15288238080 | bytes 7962624 | tf_op jit(solution)/shard_map/pallas_call | solution.py:402
  150.0 3.4 %copy.3 = f32[288,2304]{1,0:T(8,128)} copy(f32[288,2304]{1,0:T(8,128)} %shard_map.17) | data formatting | bytes 5308416
